TPU v7x, 32 devices: a whole 2x2x4 slice. The times are simulated.
32 devices in a mesh: grid: 16 (over z, y, x), col: 2 (over core).
Axes of the slice: x: 2, y: 2, z: 4, core: 2. Of those that a mesh axis runs over, the one named last changes fastest.
Arguments:
- density: bfloat16 [49152, 256], P('grid', 'col'), may hold values from -0.029907227 to 0.029907227
- row_centers: float32 [3, 49152], P(None, 'grid'), may hold values from -2 to 2
- row_exps: float32 [49152], P('grid'), may hold values from 0.2 to 1
- win_centers: float32 [3, 256], P(None, 'col'), may hold values from -2 to 2
- win_exps: float32 [256], P('col'), may hold values from 0.2 to 1
- points: float32 [64, 3, 128], P('grid'), may hold values from -2 to 2
- weights: float32 [64, 128], P('grid'), may hold values from 0.05 to 0.5
- sig_blocks: int32 [64, 32], replicated, may hold values from 0 to 383, as said below
- pair_target: int32 [64, 4096], P('grid', 'col'), may hold values from 0 to 255
- pair_source: int32 [64, 4096], P('grid', 'col'), may hold values from 0 to 127
Outputs:
- fock: float32 [49152, 256], P('grid', 'col')
Inputs may be any that keep to these rules, and one draw needn't show every extreme that they name: `sig_blocks`: each row lists 32 different blocks; block i is owned by grid index i // 24. Over the 4 rows of one grid index d (rows d * 4 to (d + 1) * 4 - 1, the batches that index holds), at most 2 different blocks of any one owner appear, and exactly 2 for some owner.
All inputs are finite; a program needn't handle non-finite values.
Results may differ from a plain program's by a relative error of at most 0.0011.
Values may be sent and summed in bfloat16 or wider, within the bound.
A program may use at most 64 MiB of HBM per device.

v0:
```python
import math

import jax
import jax.numpy as jnp
from jax import lax
from jax.sharding import PartitionSpec as P

BLK = 128
CAPB = 2


quad_nodes = 8


def boys_zero(argument):
    summed = jnp.zeros_like(argument)
    for quad_node in range(quad_nodes):
        node_spot = (quad_node + 0.5) / quad_nodes
        summed = summed + jnp.exp(-argument * (node_spot * node_spot))
    return summed / quad_nodes


def basis_values(centers, exponents, coordinates):
    squared = None
    for axis_id in range(3):
        deltas = coordinates[..., axis_id, :, None] - centers[..., axis_id, None, :]
        squared = deltas * deltas if squared is None else squared + deltas * deltas
    return jnp.exp(-exponents[..., None, :] * squared)


def pair_values(target_par, source_par, coordinates):
    target_exp = target_par[..., 3, :]
    source_exp = source_par[..., 3, :]
    joined = target_exp + source_exp
    separation = jnp.zeros_like(joined)
    spread = None
    for axis_id in range(3):
        offset = target_par[..., axis_id, :] - source_par[..., axis_id, :]
        separation = separation + offset * offset
        centre = (
            target_exp * target_par[..., axis_id, :] + source_exp * source_par[..., axis_id, :]
        ) / joined
        deltas = coordinates[..., axis_id, :, None] - centre[..., None, :]
        spread = deltas * deltas if spread is None else spread + deltas * deltas
    prefactor = 2.0 * math.pi / joined * jnp.exp(-target_exp * source_exp / joined * separation)
    return prefactor[..., None, :] * boys_zero(joined[..., None, :] * spread)


def on_device(
    density,
    row_centers,
    row_exps,
    win_centers,
    win_exps,
    points,
    weights,
    sig_blocks,
    pair_target,
    pair_source,
):
    owners = lax.axis_size("grid")
    my_index = lax.axis_index("grid")
    held_blocks = row_exps.shape[0] // BLK
    local_width = density.shape[1]
    batches_here = points.shape[0]
    listed_count = sig_blocks.shape[1]
    own_ids = my_index * held_blocks + jnp.arange(held_blocks, dtype=jnp.int32)
    every_list = sig_blocks.reshape(owners, batches_here * listed_count)
    wanted = jnp.any(every_list[:, :, None] == own_ids[None, None, :], axis=1)
    wanted_rank = jnp.cumsum(wanted.astype(jnp.int32), axis=1)
    slot_ids = jnp.arange(CAPB, dtype=jnp.int32)
    selector = wanted[:, None, :] & (wanted_rank[:, None, :] == slot_ids[None, :, None] + 1)
    own_params = jnp.concatenate([row_centers, row_exps[None, :]], axis=0).reshape(
        4, held_blocks, BLK
    )
    own_tiles = density.reshape(held_blocks, BLK, local_width)
    tile_slots = jnp.einsum(
        "dck,krw->dcrw",
        selector.astype(jnp.bfloat16),
        own_tiles,
        preferred_element_type=jnp.float32,
    ).astype(jnp.bfloat16)
    param_slots = jnp.einsum(
        "dck,xkr->dcxr", selector.astype(jnp.float32), own_params, precision=lax.Precision.HIGHEST
    )
    got_tiles = lax.all_to_all(tile_slots, "grid", split_axis=0, concat_axis=0, tiled=True)
    got_params = lax.all_to_all(param_slots, "grid", split_axis=0, concat_axis=0, tiled=True)
    my_lists = lax.dynamic_slice_in_dim(sig_blocks, my_index * batches_here, batches_here, 0)
    block_ids = jnp.arange(owners * held_blocks, dtype=jnp.int32)
    needed = jnp.any(my_lists.reshape(-1)[:, None] == block_ids[None, :], axis=0)
    needed_rank = jnp.cumsum(needed.reshape(owners, held_blocks).astype(jnp.int32), axis=1).reshape(
        -1
    )
    slot_index = my_lists // held_blocks * CAPB + jnp.take(needed_rank, my_lists) - 1
    row_tiles = got_tiles.reshape(owners * CAPB, BLK, local_width)[slot_index]
    row_tiles = row_tiles.reshape(batches_here, listed_count * BLK, local_width)
    row_params = got_params.reshape(owners * CAPB, 4, BLK)[slot_index]
    row_params = row_params.transpose(0, 2, 1, 3).reshape(batches_here, 4, listed_count * BLK)
    basis_rows = basis_values(row_params[:, 0:3], row_params[:, 3], points).astype(jnp.bfloat16)
    field_values = jnp.einsum(
        "bgf,bfw->bgw", basis_rows, row_tiles, preferred_element_type=jnp.float32
    ).astype(jnp.bfloat16)
    local_window = jnp.concatenate([win_centers, win_exps[None, :]], axis=0)
    whole_window = lax.all_gather(local_window, "col", axis=1, tiled=True)
    window_count = whole_window.shape[1]
    target_par = jnp.take(whole_window, pair_target, axis=1).transpose(1, 0, 2)
    source_par = jnp.take(local_window, pair_source, axis=1).transpose(1, 0, 2)
    source_pick = (
        pair_source[:, :, None] == jnp.arange(local_width, dtype=jnp.int32)[None, None, :]
    ).astype(jnp.bfloat16)
    target_pick = (
        pair_target[:, :, None] == jnp.arange(window_count, dtype=jnp.int32)[None, None, :]
    ).astype(jnp.bfloat16)
    field_source = jnp.einsum(
        "bgw,bnw->bgn", field_values, source_pick, preferred_element_type=jnp.float32
    )
    product = (pair_values(target_par, source_par, points) * field_source).astype(jnp.bfloat16)
    partial_sum = jnp.einsum(
        "bgn,bnw->bgw", product, target_pick, preferred_element_type=jnp.float32
    )
    potential = lax.psum_scatter(partial_sum, "col", scatter_dimension=2, tiled=True)
    weighted = (weights[:, :, None] * potential).astype(jnp.bfloat16)
    contribution_rows = jnp.einsum(
        "bgf,bgw->bfw", basis_rows, weighted, preferred_element_type=jnp.float32
    )
    contribution_rows = contribution_rows.reshape(batches_here * listed_count, BLK, local_width)
    fock_slots = (
        jnp.zeros((owners * CAPB, BLK, local_width), jnp.float32)
        .at[slot_index.reshape(-1)]
        .add(contribution_rows)
    )
    returned = lax.all_to_all(
        fock_slots.reshape(owners, CAPB, BLK, local_width),
        "grid",
        split_axis=0,
        concat_axis=0,
        tiled=True,
    )
    fock_rows = jnp.einsum(
        "dck,dcrw->krw", selector.astype(jnp.float32), returned, precision=lax.Precision.HIGHEST
    )
    return fock_rows.reshape(held_blocks * BLK, local_width)


def solution(mesh):
    return jax.shard_map(
        on_device,
        mesh=mesh,
        in_specs=(
            P("grid", "col"),
            P(None, "grid"),
            P("grid"),
            P(None, "col"),
            P("col"),
            P("grid", None, None),
            P("grid", None),
            P(),
            P("grid", "col"),
            P("grid", "col"),
        ),
        out_specs=P("grid", "col"),
        check_vma=False,
    )
```

profile of v0, /device:TPU:18, one launch (start us, length us, event | category | flops | bytes accessed | tf_op | source)
XLA Modules:
  0.0 251.3 jit_solution(6651946806612129231)
XLA Ops:
  6.5 0.8 copy.57
  7.4 0.4 compare_reduce_fusion
  7.9 0.8 copy.99
  8.7 0.2 reduce_window_sum.17
  8.8 0.9 fusion.16
  9.8 0.7 copy.59
  10.4 7.1 %all-to-all-start = ((f32[16,2,4,128]{3,2,1,0:T(4,128)}), f32[16,2,4,128]{3,2,1,0:T(4,128)S(1)}, u32[]{:S(2)}, u32[]{:S(2)}) async-start(f32[16,2,4,128]{3,2,1,0:T(4,128)} %copy.59), calls=%async_computation | async-start | bytes 131072 | tf_op jit(solution)/shard_map/all_to_all | solution.py:87
  17.5 0.8 compare_and_fusion.1
  18.3 0.8 fusion.22
  19.1 0.8 compare_and_fusion
  19.9 0.8 fusion.23
  20.6 0.7 slice_bitcast_fusion.2
  21.4 0.1 reshape.118
  21.4 0.1 eq.76
  21.5 0.1 fusion.14
  21.8 0.2 reduce_window_sum.18
  21.9 0.1 reshape.105
  22.0 1.3 gather_fusion
  23.3 0.1 reshape.117
  23.4 0.7 pad_maximum_fusion
  24.1 0.1 copy.63
  24.3 1.9 all_gather.3
  26.1 1.9 convolution_convert_fusion
  28.0 27.7 %gather_fusion.2 = f32[8192,4]{1,0:T(8,128)} fusion(f32[4,256]{0,1:T(8,128)S(1)} %all_gather.3, s32[8192]{0:T(1024)S(1)} %broadcast_clamp_fusion.1), kind=kCustom, calls=%fused_computation.2 | custom fusion | bytes 294912 | tf_op jit(solution)/shard_map/jit(_take)/gather | solution.py:106
  55.7 2.9 %copy.64 = f32[4,2048,4]{1,0,2:T(4,128)S(1)} copy(f32[4,2048,4]{2,1,0:T(8,128)} %bitcast.79) | data formatting | bytes 262144 | tf_op jit(solution)/shard_map/jit(_take)/gather | solution.py:106
  58.6 27.7 %gather_fusion.3 = f32[8192,4]{1,0:T(8,128)} fusion(f32[4,128]{0,1:T(8,128)S(1)} %copy.63, s32[8192]{0:T(1024)S(1)} %broadcast_clamp_fusion), kind=kCustom, calls=%fused_computation.3 | custom fusion | bytes 294912 | tf_op jit(solution)/shard_map/jit(_take)/gather | solution.py:107
  86.3 2.9 %copy.66 = f32[4,2048,4]{1,0,2:T(4,128)S(1)} copy(f32[4,2048,4]{2,1,0:T(8,128)} %bitcast.80) | data formatting | bytes 262144 | tf_op jit(solution)/shard_map/jit(_take)/gather | solution.py:107
  89.4 0.1 reshape.126
  89.5 1.2 copy.68
  90.7 6.9 %all-to-all-start.1 = ((bf16[16,2,128,128]{3,2,1,0:T(8,128)(2,1)}), bf16[16,2,128,128]{3,2,1,0:T(8,128)(2,1)S(1)}, u32[]{:S(2)}, u32[]{:S(2)}) async-start(bf16[16,2,128,128]{3,2,1,0:T(8,128)(2,1)} %copy.68), calls=%async_computation.1 | async-start | bytes 2097152 | tf_op jit(solution)/shard_map/all_to_all | solution.py:86
  97.7 0.8 gather_fusion.1
  98.5 0.1 reshape.108
  98.6 0.2 slice_negate_fusion
  98.8 0.1 copy_bitcast_fusion.3
  98.9 0.1 copy_bitcast_fusion.1
  99.0 23.3 %all-to-all-done.1 = bf16[16,2,128,128]{3,2,1,0:T(8,128)(2,1)S(1)} async-done(((bf16[16,2,128,128]{3,2,1,0:T(8,128)(2,1)}), bf16[16,2,128,128]{3,2,1,0:T(8,128)(2,1)S(1)}, u32[]{:S(2)}, u32[]{:S(2)}) %all-to-all-start.1) | async-done | bytes 1048608 | tf_op jit(solution)/shard_map/all_to_all | solution.py:86
  122.3 3.0 %gather_fusion.4 = bf16[128,128,128]{2,1,0:T(8,128)(2,1)} fusion(bf16[32,128,128]{2,1,0:T(8,128)(2,1)S(1)} %bitcast.77, s32[1024]{0:T(1024)S(1)} %pad_clamp_fusion), kind=kCustom, calls=%fused_computation.4 | custom fusion | bytes 8389120 | tf_op jit(solution)/shard_map/gather | solution.py:95
  125.3 13.2 %fusion.11 = bf16[4,128,128]{2,1,0:T(8,128)(2,1)S(1)} fusion(bf16[4,4096,128]{2,1,0:T(8,128)(2,1)} %bitcast.81, f32[4,4096]{1,0:T(4,128)S(1)} %get-tuple-element.21, f32[4,128]{1,0:T(4,128)S(1)} %get-tuple-element.19, f32[4,4096]{1,0:T(4,128)S(1)} %get-tuple-element.22, f32[4,128]{1,0:T(4,128)S(1)} %get-tuple-element.20, ...), kind=kOutput, calls=%fused_computation.20 | convolution fusion | flops 557907968 | bytes 4593664 | tf_op jit(solution)/shard_map/bgf,bfw->bgw/dot_general | solution.py:100
  138.5 9.0 %fusion = f32[4,128,256]{2,1,0:T(8,128)} fusion(s32[4,2048]{1,0:T(4,128)S(1)} %copy-done, f32[4,2048]{1,0:T(4,128)S(1)} %get-tuple-element.13, f32[4,2048]{1,0:T(4,128)S(1)} %get-tuple-element.12, f32[4,128]{1,0:T(4,128)S(1)} %get-tuple-element.19, f32[4,2048]{1,0:T(4,128)S(1)} %get-tuple-element.11, f32[4,128]{1,0:T(4,128)S(1)} %get-tuple-element.20, ...), kind=kOutput, calls=%fused_computation.8 | convolution fusion | flops 837812224 | bytes 890880 | tf_op jit(solution)/shard_map/bgn,bnw->bgw/dot_general | solution.py:118
  147.6 0.1 reshape.106
  147.7 8.3 %reduce-scatter.2.cloned.1.call-done = f32[4,128,128]{2,1,0:T(8,128)} async-done(((f32[4,128,256]{2,1,0:T(8,128)}), f32[4,128,128]{2,1,0:T(8,128)}) %reduce-scatter.2.cloned.1.call-update) | async-done | bytes 262160 | tf_op jit(solution)/shard_map/reduce_scatter | solution.py:121
  156.0 11.9 %fusion.3 = f32[4,4096,128]{2,1,0:T(8,128)} fusion(f32[4,4096]{1,0:T(4,128)S(1)} %get-tuple-element.21, f32[4,128]{1,0:T(4,128)S(1)} %get-tuple-element.19, f32[4,4096]{1,0:T(4,128)S(1)} %get-tuple-element.22, f32[4,128]{1,0:T(4,128)S(1)} %get-tuple-element.20, f32[4,4096]{1,0:T(4,128)S(1)} %get-tuple-element.23, f32[4,128]{1,0:T(4,128)S(1)} %get-tuple-element.18, ...), kind=kOutput, calls=%fused_computation.13 | convolution fusion | flops 557973504 | bytes 8921088 | tf_op jit(solution)/shard_map/bgf,bgw->bfw/dot_general | solution.py:123
  168.0 0.2 broadcast_in_dim.36
  168.2 17.1 %scatter_fusion = f32[32,128,128]{2,1,0:T(8,128)S(1)} fusion(f32[32,128,128]{2,1,0:T(8,128)S(1)} %broadcast_in_dim.36, s32[128]{0:T(128)S(1)} %fusion.37, f32[128,128,128]{2,1,0:T(8,128)} %bitcast.78), kind=kCustom, calls=%fused_computation.5 | custom fusion | flops 2097152 | bytes 25166336 | tf_op jit(solution)/shard_map/scatter-add | solution.py:130
  185.3 1.6 copy.70
  186.9 53.9 %all_to_all.15 = f32[16,2,128,128]{3,1,2,0:T(2,128)S(1)} all-to-all(f32[16,2,128,128]{3,1,2,0:T(2,128)S(1)} %copy.70), channel_id=1, replica_groups=mesh['grid'=16,'col'=2] {'grid'}, dimensions={0} | all-to-all | bytes 4194304 | tf_op jit(solution)/shard_map/all_to_all | solution.py:132
  240.9 2.2 fusion.8
  243.1 1.4 copy.72
  (29 shorter events, 0.5 us)
Async XLA Ops:
  10.4 80.3 %all-to-all-start = ((f32[16,2,4,128]{3,2,1,0:T(4,128)}), f32[16,2,4,128]{3,2,1,0:T(4,128)S(1)}, u32[]{:S(2)}, u32[]{:S(2)}) async-start(f32[16,2,4,128]{3,2,1,0:T(4,128)} %copy.59), calls=%async_computation | async-start | bytes 131072 | tf_op jit(solution)/shard_map/all_to_all | solution.py:87
  90.7 31.6 %all-to-all-start.1 = ((bf16[16,2,128,128]{3,2,1,0:T(8,128)(2,1)}), bf16[16,2,128,128]{3,2,1,0:T(8,128)(2,1)S(1)}, u32[]{:S(2)}, u32[]{:S(2)}) async-start(bf16[16,2,128,128]{3,2,1,0:T(8,128)(2,1)} %copy.68), calls=%async_computation.1 | async-start | bytes 2097152 | tf_op jit(solution)/shard_map/all_to_all | solution.py:86
  97.7 58.4 %reduce-scatter.2.cloned.1.call-start = ((), (), s32[]{:S(2)}) async-start(), calls=%async_computation.4 | async-start | bytes 786432 | tf_op jit(solution)/shard_map/reduce_scatter | solution.py:121
  125.3 13.2 %copy-start = (s32[4,2048]{1,0:T(4,128)S(1)}, s32[4,2048]{1,0:T(4,128)}, u32[]{:S(2)}) copy-start(s32[4,2048]{1,0:T(4,128)} %param.18) | copy-start | bytes 98308
  125.3 13.2 %copy-start.1 = (s32[4,2048]{1,0:T(4,128)S(1)}, s32[4,2048]{1,0:T(4,128)}, u32[]{:S(2)}) copy-start(s32[4,2048]{1,0:T(4,128)} %param.19) | copy-start | bytes 98308
  138.5 17.5 %copy-start.2 = (f32[4,128]{1,0:T(4,128)S(1)}, f32[4,128]{1,0:T(4,128)}, u32[]{:S(2)}) copy-start(f32[4,128]{1,0:T(4,128)} %param.16) | copy-start | bytes 6148
Sparse Core Ops, SparseCore 0:
  147.7 8.2 reduce-scatter.1
where the time goes:
time: 256 us; the launch traced here: 251 us
  local copies, waits for them, and re-layouts  74.8 us (29%)
  blocking collectives  55.8 us (22%)
  matrix products  39.1 us (15%)
  waiting for transfers between devices  31.7 us (12%)
  other arithmetic  22.3 us (9%)
  starting transfers between devices  14 us (5%)
  between operations  13.7 us (5%)
    all_to_all x1, blocking collectives, on_device(): lax.all_to_all(fock_slots.reshape(owners, CAPB, BLK, local_width), 'grid'...  53.9 us
    gather x2, local copies, waits for them, and re-layouts, on_device(): target_par = jnp.take(whole_window, pair_target, axis=1).transpose(1, 0, 2)  30.6 us
    gather x2, local copies, waits for them, and re-layouts, on_device(): source_par = jnp.take(local_window, pair_source, axis=1).transpose(1, 0, 2)  30.6 us
    all_to_all x1, waiting for transfers between devices, on_device(): lax.all_to_all(tile_slots, 'grid', split_axis=0, concat_axis=0, tiled=True)  23.3 us
    scatter-add x1, other arithmetic, on_device(): fock_slots = jnp.zeros((owners * CAPB, BLK, local_width), jnp.float32).at...  17.1 us
    dot_general x1, matrix products, on_device(): jnp.einsum('bgf,bfw->bgw', basis_rows, row_tiles, preferred_element_type=...  13.2 us
    dot_general x1, matrix products, on_device(): jnp.einsum('bgf,bgw->bfw', basis_rows, weighted, preferred_element_type=j...  11.9 us
    dot_general x1, matrix products, on_device(): jnp.einsum('bgn,bnw->bgw', product, target_pick, preferred_element_type=j...  9.04 us
  transfers between devices with their start and end apart: 3, of which 2 were waited for; matrix products, arithmetic and copies ran while one was open for 29% of the time, Pallas kernels for 0%

commit v1 on v0

v1 whole, which is shorter than its diff:
```python
import functools
import math

import jax
import jax.numpy as jnp
from jax import lax
from jax.experimental import pallas as pl
from jax.experimental.pallas import tpu as pltpu
from jax.sharding import PartitionSpec as P

BLK = 128
CAPB = 2
MESH = pl.DeviceIdType.MESH
VMEM_LIMIT = 52 * 1024 * 1024

quad_nodes = 8


def boys_sum(argument):
    first = jnp.exp(argument * (-0.25 / (quad_nodes * quad_nodes)))
    ratio = jnp.exp(argument * (-2.0 / (quad_nodes * quad_nodes)))
    powers = [ratio]
    for _ in range(quad_nodes - 2):
        powers.append(powers[-1] * ratio)
    summed = 1.0 + powers[-1]
    for power in powers[-2::-1]:
        summed = 1.0 + power * summed
    return first * summed


def three_pieces(values):
    high = values.astype(jnp.bfloat16).astype(jnp.float32)
    rest = values - high
    middle = rest.astype(jnp.bfloat16).astype(jnp.float32)
    return jnp.concatenate([high, middle, rest - middle], axis=0).astype(jnp.bfloat16)


def picked(pieces, pick):
    out = jnp.dot(pieces, pick, preferred_element_type=jnp.float32)
    return out[0:8] + out[8:16] + out[16:24]


def one_hot(ids, count):
    rows = lax.broadcasted_iota(jnp.int32, (count, ids.shape[1]), 0)
    return jnp.where(rows == ids, 1.0, 0.0).astype(jnp.bfloat16)


def exchange_kernel(
    owners, cols, full,
    slot_ref, mask_ref, density_ref, params_ref, win_c_ref, win_e_ref, points_ref, weights_ref,
    target_ref, source_ref,
    weighted_ref, all_points_ref,
    tile_send, tile_recv, msg_send, msg_recv, win_buf, spots, pair_scr, source_hot, target_hot, field, parts, parts_recv,
    tile_ss, tile_rs, msg_ss, msg_rs, win_ss, win_rs, part_ss, part_rs,
):
    me = lax.axis_index("grid")
    mc = lax.axis_index("col")
    batches, pairs = target_ref.shape
    pts = points_ref.shape[2]
    width = density_ref.shape[2]
    window = cols * width
    chunk = 256

    barrier = pltpu.get_barrier_semaphore()

    def greet_grid(j, carry):
        pl.semaphore_signal(
            barrier, inc=1, device_id={"grid": lax.rem(me + j, owners), "col": mc}, device_id_type=MESH
        )
        return carry

    def greet_col(j, carry):
        pl.semaphore_signal(
            barrier, inc=1, device_id={"grid": me, "col": lax.rem(mc + j, cols)}, device_id_type=MESH
        )
        return carry

    lax.fori_loop(1, owners, greet_grid, 0)
    lax.fori_loop(1, cols, greet_col, 0)

    def win_copy(j):
        return pltpu.make_async_remote_copy(
            src_ref=win_buf.at[mc], dst_ref=win_buf.at[mc], send_sem=win_ss.at[j], recv_sem=win_rs.at[j],
            device_id={"grid": me, "col": lax.rem(mc + j, cols)}, device_id_type=MESH,
        )

    def win_arrival(j):
        there = lax.rem(mc - j + cols, cols)
        return pltpu.make_async_remote_copy(
            src_ref=win_buf.at[there], dst_ref=win_buf.at[there], send_sem=win_ss.at[j], recv_sem=win_rs.at[j],
            device_id={"grid": me, "col": lax.rem(mc + j, cols)}, device_id_type=MESH,
        )

    def msg_copy(j):
        return pltpu.make_async_remote_copy(
            src_ref=msg_send.at[j], dst_ref=msg_recv.at[j], send_sem=msg_ss.at[j], recv_sem=msg_rs.at[j],
            device_id={"grid": lax.rem(me + j, owners), "col": mc}, device_id_type=MESH,
        )

    def tile_copy(j):
        return pltpu.make_async_remote_copy(
            src_ref=tile_send.at[j], dst_ref=tile_recv.at[j], send_sem=tile_ss.at[j], recv_sem=tile_rs.at[j],
            device_id={"grid": lax.rem(me + j, owners), "col": mc}, device_id_type=MESH,
        )

    def part_copy(j):
        there = lax.rem(mc + j, cols)
        return pltpu.make_async_remote_copy(
            src_ref=parts.at[there], dst_ref=parts_recv.at[j], send_sem=part_ss.at[j], recv_sem=part_rs.at[j],
            device_id={"grid": me, "col": there}, device_id_type=MESH,
        )

    own_win = jnp.concatenate([win_c_ref[...], win_e_ref[...], jnp.zeros((4, width), jnp.float32)], axis=0)
    win_buf[mc] = own_win
    own_points = jnp.concatenate([points_ref[b] for b in range(batches)] + [weights_ref[...]], axis=0)

    def stage(j, tile_to, msg_to, index):
        peer = lax.rem(me + j, owners)
        rows = []
        for c in range(CAPB):
            block = slot_ref[peer * CAPB + c]
            tile_to[index, c * BLK : (c + 1) * BLK] = density_ref[block]
            rows.append(params_ref[block])
        msg_to[index] = jnp.concatenate(rows + [own_points], axis=0)

    stage(0, tile_recv, msg_recv, 0)
    pl.semaphore_wait(barrier, owners - 1 + cols - 1)

    for j in range(1, cols):
        win_copy(j).start()

    def send(j, carry):
        stage(j, tile_send, msg_send, j)
        msg_copy(j).start()
        tile_copy(j).start()
        return carry

    lax.fori_loop(1, owners, send, 0)

    columns = own_points.T
    for b in range(batches):
        for a in range(3):
            spots[a, b * pts : (b + 1) * pts] = jnp.broadcast_to(columns[:, 3 * b + a : 3 * b + a + 1], (pts, BLK))
        at = 3 * batches + b
        spots[3, b * pts : (b + 1) * pts] = jnp.broadcast_to(columns[:, at : at + 1], (pts, BLK))

    for j in range(1, cols):
        win_arrival(j).wait_recv()
    source_pieces = three_pieces(own_win)
    target_pieces = three_pieces(jnp.concatenate([win_buf[k] for k in range(cols)], axis=1))
    per_batch = pairs // chunk

    def pair_step(i, carry):
        b = i // per_batch
        lanes = pl.ds(pl.multiple_of(lax.rem(i, per_batch) * chunk, chunk), chunk)
        rows = pl.ds(pl.multiple_of(b * pts, pts), pts)
        target_pick = one_hot(target_ref[pl.ds(b, 1), lanes], window)
        source_pick = one_hot(source_ref[pl.ds(b, 1), lanes], width)
        target_hot[b, :, lanes] = target_pick
        source_hot[b, :, lanes] = source_pick
        tp = picked(target_pieces, target_pick)
        sp = picked(source_pieces, source_pick)
        te, se = tp[3:4], sp[3:4]
        joined = te + se
        separation = jnp.zeros_like(joined)
        centre = []
        for a in range(3):
            offset = tp[a : a + 1] - sp[a : a + 1]
            separation = separation + offset * offset
            centre.append((te * tp[a : a + 1] + se * sp[a : a + 1]) / joined)
        prefactor = (2.0 * math.pi / quad_nodes) / joined * jnp.exp(-te * se / joined * separation)
        out = []
        for h in range(chunk // BLK):
            part = slice(h * BLK, (h + 1) * BLK)
            spread = None
            for a in range(3):
                deltas = spots[a, rows] - centre[a][:, part]
                spread = deltas * deltas if spread is None else spread + deltas * deltas
            out.append(prefactor[:, part] * boys_sum(joined[:, part] * spread))
        pair_scr[rows, lanes] = jnp.concatenate(out, axis=1)
        return carry

    lax.fori_loop(0, batches * per_batch, pair_step, 0)

    field[...] = jnp.zeros_like(field)

    def add_field(j):
        owner = lax.rem(me - j + owners, owners)
        params = msg_recv[j]
        all_points_ref[owner] = params[8:24]
        tile = tile_recv[j]
        for b in range(batches):
            rows = slice(b * pts, (b + 1) * pts)
            halves = []
            for c in range(CAPB):
                squared = None
                for a in range(3):
                    deltas = spots[a, rows] - params[4 * c + a : 4 * c + a + 1]
                    squared = deltas * deltas if squared is None else squared + deltas * deltas
                value = jnp.exp(-params[4 * c + 3 : 4 * c + 4] * squared)
                if not full:
                    value = value * mask_ref[(b * owners + owner) * CAPB + c]
                halves.append(value.astype(jnp.bfloat16))
            basis = jnp.concatenate(halves, axis=1)
            field[rows] += jnp.dot(basis, tile, preferred_element_type=jnp.float32)

    add_field(0)

    def take(j, carry):
        msg_copy(j).wait_recv()
        tile_copy(j).wait_recv()
        add_field(j)
        return carry

    lax.fori_loop(1, owners, take, 0)

    def batch_step(b, carry):
        rows = pl.ds(pl.multiple_of(b * pts, pts), pts)
        values = field[rows].astype(jnp.bfloat16)
        total = jnp.zeros((pts, window), jnp.float32)
        for i in range(per_batch // 2):
            lanes = slice(i * 2 * chunk, (i + 1) * 2 * chunk)
            from_field = jnp.dot(values, source_hot[b, :, lanes], preferred_element_type=jnp.float32)
            product = (pair_scr[rows, lanes] * from_field).astype(jnp.bfloat16)
            total = total + lax.dot_general(
                product, target_hot[b, :, lanes], (((1,), (1,)), ((), ())), preferred_element_type=jnp.float32
            )
        for k in range(cols):
            parts[k, rows] = total[:, k * width : (k + 1) * width]
        return carry

    lax.fori_loop(0, batches, batch_step, 0)

    for j in range(1, cols):
        part_copy(j).start()
    for j in range(1, cols):
        part_copy(j).wait_recv()
    potential = parts[mc]
    for j in range(1, cols):
        potential = potential + parts_recv[j]
    weighted_ref[...] = (spots[3] * potential).astype(jnp.bfloat16)

    for j in range(1, cols):
        win_copy(j).wait_send()
        part_copy(j).wait_send()

    def drain(j, carry):
        msg_copy(j).wait_send()
        tile_copy(j).wait_send()
        return carry

    lax.fori_loop(1, owners, drain, 0)


def fock_kernel(owners, batches, full, slot_ref, mask_ref, weighted_ref, points_ref, params_ref, fock_ref):
    fock_ref[...] = jnp.zeros_like(fock_ref)
    count = weighted_ref.shape[0] // owners
    blank = jnp.zeros((4, BLK), jnp.float32)

    def step(user, carry):
        weighted = weighted_ref[pl.ds(pl.multiple_of(user * count, count), count), :]
        spot = points_ref[user]
        for c in range(CAPB):
            block = slot_ref[user * CAPB + c]
            params = jnp.concatenate([params_ref[block], blank], axis=0).T
            held = [jnp.broadcast_to(params[:, a : a + 1], (BLK, BLK)) for a in range(4)]
            basis = []
            for b in range(batches):
                squared = None
                for a in range(3):
                    deltas = spot[3 * b + a : 3 * b + a + 1] - held[a]
                    squared = deltas * deltas if squared is None else squared + deltas * deltas
                value = jnp.exp(-held[3] * squared)
                if not full:
                    value = value * mask_ref[(user * CAPB + c) * batches + b]
                basis.append(value.astype(jnp.bfloat16))
            fock_ref[block] += jnp.dot(
                jnp.concatenate(basis, axis=1), weighted, preferred_element_type=jnp.float32
            )
        return carry

    lax.fori_loop(0, owners, step, 0)


def on_device(
    density, row_centers, row_exps, win_centers, win_exps, points, weights, sig_blocks, pair_target, pair_source
):
    owners = lax.axis_size("grid")
    cols = lax.axis_size("col")
    me = lax.axis_index("grid")
    rows_here = row_exps.shape[0]
    held = rows_here // BLK
    width = density.shape[1]
    batches, _, pts = points.shape
    pairs = pair_target.shape[1]
    listed = sig_blocks.shape[1]
    full = listed == owners * CAPB
    count = batches * pts

    lists = sig_blocks.reshape(owners, batches * listed)
    local = lists - me * held
    mine = (local >= 0) & (local < held)
    low = jnp.min(jnp.where(mine, local, held), axis=1)
    high = jnp.max(jnp.where(mine, local, -1), axis=1)
    slots = jnp.clip(jnp.stack([low, high], axis=1), 0, held - 1).reshape(-1)
    if full:
        user_mask = owner_mask = jnp.zeros((1,), jnp.float32)
    else:
        my_lists = lax.dynamic_slice_in_dim(sig_blocks, me * batches, batches, 0)
        flat = my_lists.reshape(1, -1)
        of_owner = flat // held == jnp.arange(owners, dtype=jnp.int32)[:, None]
        least = jnp.min(jnp.where(of_owner, flat, owners * held), axis=1)
        most = jnp.max(jnp.where(of_owner, flat, -1), axis=1)
        most = jnp.where(most == least, -1, most)
        wanted = jnp.stack([least, most], axis=1)
        user_mask = jnp.any(my_lists[:, :, None, None] == wanted, axis=1).astype(jnp.float32).reshape(-1)
        ids = jnp.stack([low, jnp.where(high == low, -1, high)], axis=1)
        ids = jnp.where((ids >= 0) & (ids < held), ids + me * held, -1)
        by_batch = sig_blocks.reshape(owners, 1, batches, listed)
        owner_mask = jnp.any(by_batch == ids[:, :, None, None], axis=3).astype(jnp.float32).reshape(-1)

    smem = pl.BlockSpec(memory_space=pltpu.SMEM)
    vmem = pl.BlockSpec(memory_space=pltpu.VMEM)
    own_tiles = density.reshape(held, BLK, width)
    params = jnp.concatenate([row_centers, row_exps[None, :]], axis=0).reshape(4, held, BLK).transpose(1, 0, 2)
    weighted, all_points = pl.pallas_call(
        functools.partial(exchange_kernel, owners, cols, full),
        out_shape=(
            jax.ShapeDtypeStruct((count, width), jnp.bfloat16),
            jax.ShapeDtypeStruct((owners, 16, pts), jnp.float32),
        ),
        in_specs=[smem, smem] + [vmem] * 8,
        out_specs=(vmem, vmem),
        scratch_shapes=[
            pltpu.VMEM((owners, CAPB * BLK, width), jnp.bfloat16),
            pltpu.VMEM((owners, CAPB * BLK, width), jnp.bfloat16),
            pltpu.VMEM((owners, 24, BLK), jnp.float32),
            pltpu.VMEM((owners, 24, BLK), jnp.float32),
            pltpu.VMEM((cols, 8, width), jnp.float32),
            pltpu.VMEM((4, count, BLK), jnp.float32),
            pltpu.VMEM((count, pairs), jnp.float32),
            pltpu.VMEM((batches, width, pairs), jnp.bfloat16),
            pltpu.VMEM((batches, cols * width, pairs), jnp.bfloat16),
            pltpu.VMEM((count, width), jnp.float32),
            pltpu.VMEM((cols, count, width), jnp.float32),
            pltpu.VMEM((cols, count, width), jnp.float32),
            pltpu.SemaphoreType.DMA((owners,)),
            pltpu.SemaphoreType.DMA((owners,)),
            pltpu.SemaphoreType.DMA((owners,)),
            pltpu.SemaphoreType.DMA((owners,)),
            pltpu.SemaphoreType.DMA((cols,)),
            pltpu.SemaphoreType.DMA((cols,)),
            pltpu.SemaphoreType.DMA((cols,)),
            pltpu.SemaphoreType.DMA((cols,)),
        ],
        compiler_params=pltpu.CompilerParams(
            collective_id=0, has_side_effects=True, vmem_limit_bytes=VMEM_LIMIT
        ),
        name="exchange",
    )(
        slots, user_mask, own_tiles, params, win_centers, win_exps[None, :], points, weights,
        pair_target, pair_source,
    )
    every = lax.all_gather(weighted, "grid", axis=0, tiled=True)
    return pl.pallas_call(
        functools.partial(fock_kernel, owners, batches, full),
        out_shape=jax.ShapeDtypeStruct((held, BLK, width), jnp.float32),
        in_specs=[smem, smem] + [vmem] * 3,
        out_specs=vmem,
        compiler_params=pltpu.CompilerParams(vmem_limit_bytes=VMEM_LIMIT),
        name="fock_rows",
    )(slots, owner_mask, every, all_points, params).reshape(rows_here, width)


def solution(mesh):
    return jax.shard_map(
        on_device,
        mesh=mesh,
        in_specs=(
            P("grid", "col"),
            P(None, "grid"),
            P("grid"),
            P(None, "col"),
            P("col"),
            P("grid", None, None),
            P("grid", None),
            P(),
            P("grid", "col"),
            P("grid", "col"),
        ),
        out_specs=P("grid", "col"),
        check_vma=False,
    )
```

time: 256 us -> 137 us (0.54)
  the two profiles are of different devices: /device:TPU:18 before, /device:TPU:0 now
where the time goes in v1:
time: 137 us
  waiting for transfers between devices  69.9 us (51%)
  Pallas kernels  46 us (34%)
  between operations  13.4 us (10%)
  local copies, waits for them, and re-layouts  5.69 us (4%)
  other arithmetic  1.84 us (1%)
    all_gather x1, waiting for transfers between devices, on_device(): every = lax.all_gather(weighted, 'grid', axis=0, tiled=True)  69.9 us
    pallas_call x1, Pallas kernels, on_device(): pl.pallas_call(functools.partial(exchange_kernel, owners, cols, full), ou...  34.1 us
    pallas_call x1, Pallas kernels, on_device(): pl.pallas_call(functools.partial(fock_kernel, owners, batches, full), out...  11.9 us
    unnamed x13, local copies, waits for them, and re-layouts  5.36 us
  transfers between devices with their start and end apart: 1, of which 1 were waited for; matrix products, arithmetic and copies ran while one was open for 0% of the time, Pallas kernels for 0%

profile of v1, /device:TPU:0, one launch (start us, length us, event | category | flops | bytes accessed | tf_op | source)
XLA Modules:
  0.0 136.9 jit_solution(16790905827298898833)
XLA Ops:
  6.5 0.0 all-gather.2.cloned.1.call-start
  6.5 0.7 select_reduce_fusion.1
  7.3 0.1 reduce_min.14
  7.4 0.1 reduce_max.14
  7.4 0.1 reduce_min.18
  7.6 0.1 reduce_max.18
  7.7 0.1 copy.13
  7.8 0.1 min.12.slot_ref
  7.9 0.7 copy.14.points_ref
  8.6 0.8 maximum_bitcast_fusion.params_ref
  9.4 0.0 copy-start
  9.4 1.1 copy-done
  10.6 0.0 copy-start.1
  10.6 0.8 copy-done.1
  11.3 0.0 copy-start.2
  11.3 0.8 copy-done.2
  12.1 0.0 copy-start.3
  12.1 0.7 copy-done.3
  12.8 0.0 copy-start.4
  12.8 0.7 copy-done.4
  13.4 0.0 copy-start.5
  13.4 0.7 copy-done.5
  14.1 34.1 %exchange.1 = (bf16[512,128]{1,0:T(8,128)(2,1)}, f32[16,16,128]{2,1,0:T(8,128)S(1)}) custom-call(s32[32]{0:T(128)S(1)} %min.12.slot_ref, f32[1]{0:T(128)} %constant.8.clone.1.mask_ref, bf16[24,128,128]{2,1,0:T(8,128)(2,1)S(1)} %bitcast.9, f32[24,4,128]{2,1,0:T(4,128)S(1)} %maximum_bitcast_fusion.params_ref, f32[3,128]{1,0:T(4,128)S(1)} %copy-done.3, ...), custom_call_target="tpu_custom_call" | custom-call | tf_op jit(solution)/shard_map/exchange/pallas_call | solution.py:326
  48.2 0.0 all-gather.2.cloned.1.call-update
  48.2 69.9 %all-gather.2.cloned.1.call-done.weighted_ref = bf16[8192,128]{1,0:T(8,128)(2,1)} async-done(((bf16[512,128]{1,0:T(8,128)(2,1)}), bf16[8192,128]{1,0:T(8,128)(2,1)}) %all-gather.2.cloned.1.call-update) | async-done | bytes 2097168 | tf_op jit(solution)/shard_map/all_gather | solution.py:364
  118.1 11.9 %fock_rows.1 = f32[24,128,128]{2,1,0:T(8,128)} custom-call(s32[32]{0:T(128)S(1)} %min.12.slot_ref, f32[1]{0:T(128)} %constant.8.clone.1.mask_ref, bf16[8192,128]{1,0:T(8,128)(2,1)} %all-gather.2.cloned.1.call-done.weighted_ref, f32[16,16,128]{2,1,0:T(8,128)S(1)} %get-tuple-element.8.points_ref, f32[24,4,128]{2,1,0:T(4,128)S(1)} %maximum_bitcast_fusion.params_ref), custom_call_target="tpu_custom_call" | custom-call | tf_op jit(solution)/shard_map/fock_rows/pallas_call | solution.py:365
  (1 shorter events, 0.0 us)
Async XLA Ops:
  6.5 111.6 %all-gather.2.cloned.1.call-start = ((), (), s32[]{:S(2)}) async-start(), calls=%async_computation | async-start | bytes 2228224 | tf_op jit(solution)/shard_map/all_gather | solution.py:364
  9.4 1.1 copy-start
  10.6 0.8 copy-start.1
  11.3 0.8 copy-start.2
  12.1 0.7 copy-start.3
  12.8 0.7 copy-start.4
  13.4 0.7 copy-start.5
Sparse Core Ops, SparseCore 0:
  48.3 69.7 all-gather.1

commit v2 on v1

--- a/solution.py
+++ b/solution.py
@@ -11,7 +11,7 @@
 BLK = 128
 CAPB = 2
 MESH = pl.DeviceIdType.MESH
-VMEM_LIMIT = 52 * 1024 * 1024
+VMEM_LIMIT = 57 * 1024 * 1024
 
 quad_nodes = 8
 
@@ -47,11 +47,11 @@
 
 def exchange_kernel(
     owners, cols, full,
-    slot_ref, mask_ref, density_ref, params_ref, win_c_ref, win_e_ref, points_ref, weights_ref,
+    slot_ref, mask_ref, owner_mask_ref, density_ref, params_ref, win_c_ref, win_e_ref, points_ref, weights_ref,
     target_ref, source_ref,
-    weighted_ref, all_points_ref,
-    tile_send, tile_recv, msg_send, msg_recv, win_buf, spots, pair_scr, source_hot, target_hot, field, parts, parts_recv,
-    tile_ss, tile_rs, msg_ss, msg_rs, win_ss, win_rs, part_ss, part_rs,
+    partial_ref,
+    every, all_points, tile_send, tile_recv, msg_send, msg_recv, win_buf, spots, pair_scr, source_hot, target_hot, field, parts, parts_recv,
+    tile_ss, tile_rs, msg_ss, msg_rs, win_ss, win_rs, part_ss, part_rs, every_ss, every_rs,
 ):
     me = lax.axis_index("grid")
     mc = lax.axis_index("col")
@@ -60,6 +60,10 @@
     width = density_ref.shape[2]
     window = cols * width
     chunk = 256
+    x, y, z = lax.rem(me, 2), lax.rem(me // 2, 2), me // 4
+    deep = owners // 4
+    half_batches = batches // 2
+    half = half_batches * pts
 
     barrier = pltpu.get_barrier_semaphore()
 
@@ -103,12 +107,56 @@
             device_id={"grid": lax.rem(me + j, owners), "col": mc}, device_id_type=MESH,
         )
 
-    def part_copy(j):
+    def part_copy(j, h):
         there = lax.rem(mc + j, cols)
-        return pltpu.make_async_remote_copy(
-            src_ref=parts.at[there], dst_ref=parts_recv.at[j], send_sem=part_ss.at[j], recv_sem=part_rs.at[j],
-            device_id={"grid": me, "col": there}, device_id_type=MESH,
-        )
+        rows = slice(h * half, (h + 1) * half)
+        return pltpu.make_async_remote_copy(
+            src_ref=parts.at[there, rows], dst_ref=parts_recv.at[j, rows], send_sem=part_ss.at[j, h],
+            recv_sem=part_rs.at[j, h], device_id={"grid": me, "col": there}, device_id_type=MESH,
+        )
+
+    def spread_copy(user, h, peer, way):
+        return pltpu.make_async_remote_copy(
+            src_ref=every.at[user, h], dst_ref=every.at[user, h], send_sem=every_ss.at[way, h],
+            recv_sem=every_rs.at[user, h], device_id={"grid": peer, "col": mc}, device_id_type=MESH,
+        )
+
+    def place(k, across_y, across_x):
+        there_y = 1 - y if across_y else y
+        there_x = 1 - x if across_x else x
+        return (lax.rem(z + k, deep) * 2 + there_y) * 2 + there_x
+
+    def send_x(user, h):
+        spread_copy(user, h, place(0, False, True), 0).start()
+
+    def send_y(user, h):
+        spread_copy(user, h, place(0, True, False), 1).start()
+
+    def arrived(user, h):
+        spread_copy(user, h, place(0, False, True), 0).wait_recv()
+
+    blank = jnp.zeros((4, BLK), jnp.float32)
+
+    def add_fock(user, h):
+        weighted = every[user, h]
+        spot = all_points[user]
+        for c in range(CAPB):
+            block = slot_ref[user * CAPB + c]
+            own = jnp.concatenate([params_ref[block], blank], axis=0).T
+            held = [jnp.broadcast_to(own[:, a : a + 1], (BLK, BLK)) for a in range(4)]
+            basis = []
+            for b in range(h * half_batches, (h + 1) * half_batches):
+                squared = None
+                for a in range(3):
+                    deltas = spot[3 * b + a : 3 * b + a + 1] - held[a]
+                    squared = deltas * deltas if squared is None else squared + deltas * deltas
+                value = jnp.exp(-held[3] * squared)
+                if not full:
+                    value = value * owner_mask_ref[(user * CAPB + c) * batches + b]
+                basis.append(value.astype(jnp.bfloat16))
+            partial_ref[user * CAPB + c] += jnp.dot(
+                jnp.concatenate(basis, axis=1), weighted, preferred_element_type=jnp.float32
+            )
 
     own_win = jnp.concatenate([win_c_ref[...], win_e_ref[...], jnp.zeros((4, width), jnp.float32)], axis=0)
     win_buf[mc] = own_win
@@ -183,11 +231,12 @@
     lax.fori_loop(0, batches * per_batch, pair_step, 0)
 
     field[...] = jnp.zeros_like(field)
+    partial_ref[...] = jnp.zeros_like(partial_ref)
 
     def add_field(j):
         owner = lax.rem(me - j + owners, owners)
         params = msg_recv[j]
-        all_points_ref[owner] = params[8:24]
+        all_points[owner] = params[8:24]
         tile = tile_recv[j]
         for b in range(batches):
             rows = slice(b * pts, (b + 1) * pts)
@@ -229,20 +278,78 @@
             parts[k, rows] = total[:, k * width : (k + 1) * width]
         return carry
 
-    lax.fori_loop(0, batches, batch_step, 0)
-
-    for j in range(1, cols):
-        part_copy(j).start()
-    for j in range(1, cols):
-        part_copy(j).wait_recv()
-    potential = parts[mc]
-    for j in range(1, cols):
-        potential = potential + parts_recv[j]
-    weighted_ref[...] = (spots[3] * potential).astype(jnp.bfloat16)
+    for h in range(2):
+        lax.fori_loop(h * half_batches, (h + 1) * half_batches, batch_step, 0)
+        for j in range(1, cols):
+            part_copy(j, h).start()
+    for h in range(2):
+        rows = slice(h * half, (h + 1) * half)
+        for j in range(1, cols):
+            part_copy(j, h).wait_recv()
+        potential = parts[mc, rows]
+        for j in range(1, cols):
+            potential = potential + parts_recv[j, rows]
+        every[me, h] = (spots[3, rows] * potential).astype(jnp.bfloat16)
+        send_x(me, h)
+        send_y(me, h)
+        for k in range(1, deep):
+            spread_copy(me, h, place(k, False, False), 2).start()
+
+    def forward_side(k):
+        arrived(place(k, False, True), 0)
+        send_y(place(k, False, True), 0)
+        arrived(place(k, True, False), 1)
+        send_x(place(k, True, False), 1)
+
+    def add_side(k):
+        add_fock(place(k, False, True), 0)
+        add_fock(place(k, True, False), 1)
+
+    add_fock(me, 0)
+    add_fock(me, 1)
+
+    def relay(k, carry):
+        user = place(k, False, False)
+        for h in range(2):
+            arrived(user, h)
+            send_x(user, h)
+            send_y(user, h)
+        forward_side(k - 1)
+        add_fock(user, 0)
+        add_fock(user, 1)
+        add_side(k - 1)
+        return carry
+
+    lax.fori_loop(1, deep, relay, 0)
+    forward_side(deep - 1)
+    add_side(deep - 1)
+
+    def last(k, carry):
+        near = place(k, True, False), place(k, False, True)
+        for h in range(2):
+            arrived(near[h], h)
+            add_fock(near[h], h)
+        far = place(k, True, True)
+        for h in range(2):
+            arrived(far, h)
+            add_fock(far, h)
+        return carry
+
+    lax.fori_loop(0, deep, last, 0)
 
     for j in range(1, cols):
         win_copy(j).wait_send()
-        part_copy(j).wait_send()
+        for h in range(2):
+            part_copy(j, h).wait_send()
+
+    for h in range(2):
+        for way, sent in ((h, deep), (1 - h, 2 * deep), (2, deep - 1)):
+
+            def drain_spread(k, carry, h=h, way=way):
+                spread_copy(me, h, place(0, False, True), way).wait_send()
+                return carry
+
+            lax.fori_loop(0, sent, drain_spread, 0)
 
     def drain(j, carry):
         msg_copy(j).wait_send()
@@ -252,34 +359,14 @@
     lax.fori_loop(1, owners, drain, 0)
 
 
-def fock_kernel(owners, batches, full, slot_ref, mask_ref, weighted_ref, points_ref, params_ref, fock_ref):
+def fock_kernel(slot_ref, partial_ref, fock_ref):
     fock_ref[...] = jnp.zeros_like(fock_ref)
-    count = weighted_ref.shape[0] // owners
-    blank = jnp.zeros((4, BLK), jnp.float32)
-
-    def step(user, carry):
-        weighted = weighted_ref[pl.ds(pl.multiple_of(user * count, count), count), :]
-        spot = points_ref[user]
-        for c in range(CAPB):
-            block = slot_ref[user * CAPB + c]
-            params = jnp.concatenate([params_ref[block], blank], axis=0).T
-            held = [jnp.broadcast_to(params[:, a : a + 1], (BLK, BLK)) for a in range(4)]
-            basis = []
-            for b in range(batches):
-                squared = None
-                for a in range(3):
-                    deltas = spot[3 * b + a : 3 * b + a + 1] - held[a]
-                    squared = deltas * deltas if squared is None else squared + deltas * deltas
-                value = jnp.exp(-held[3] * squared)
-                if not full:
-                    value = value * mask_ref[(user * CAPB + c) * batches + b]
-                basis.append(value.astype(jnp.bfloat16))
-            fock_ref[block] += jnp.dot(
-                jnp.concatenate(basis, axis=1), weighted, preferred_element_type=jnp.float32
-            )
-        return carry
-
-    lax.fori_loop(0, owners, step, 0)
+
+    def step(i, carry):
+        fock_ref[slot_ref[i]] += partial_ref[i]
+        return carry
+
+    lax.fori_loop(0, partial_ref.shape[0], step, 0)
 
 
 def on_device(
@@ -323,15 +410,14 @@
     vmem = pl.BlockSpec(memory_space=pltpu.VMEM)
     own_tiles = density.reshape(held, BLK, width)
     params = jnp.concatenate([row_centers, row_exps[None, :]], axis=0).reshape(4, held, BLK).transpose(1, 0, 2)
-    weighted, all_points = pl.pallas_call(
+    partial = pl.pallas_call(
         functools.partial(exchange_kernel, owners, cols, full),
-        out_shape=(
-            jax.ShapeDtypeStruct((count, width), jnp.bfloat16),
-            jax.ShapeDtypeStruct((owners, 16, pts), jnp.float32),
-        ),
-        in_specs=[smem, smem] + [vmem] * 8,
-        out_specs=(vmem, vmem),
+        out_shape=jax.ShapeDtypeStruct((owners * CAPB, BLK, width), jnp.float32),
+        in_specs=[smem, smem, smem] + [vmem] * 8,
+        out_specs=vmem,
         scratch_shapes=[
+            pltpu.VMEM((owners, 2, count // 2, width), jnp.bfloat16),
+            pltpu.VMEM((owners, 16, pts), jnp.float32),
             pltpu.VMEM((owners, CAPB * BLK, width), jnp.bfloat16),
             pltpu.VMEM((owners, CAPB * BLK, width), jnp.bfloat16),
             pltpu.VMEM((owners, 24, BLK), jnp.float32),
@@ -350,26 +436,27 @@
             pltpu.SemaphoreType.DMA((owners,)),
             pltpu.SemaphoreType.DMA((cols,)),
             pltpu.SemaphoreType.DMA((cols,)),
-            pltpu.SemaphoreType.DMA((cols,)),
-            pltpu.SemaphoreType.DMA((cols,)),
+            pltpu.SemaphoreType.DMA((cols, 2)),
+            pltpu.SemaphoreType.DMA((cols, 2)),
+            pltpu.SemaphoreType.DMA((3, 2)),
+            pltpu.SemaphoreType.DMA((owners, 2)),
         ],
         compiler_params=pltpu.CompilerParams(
             collective_id=0, has_side_effects=True, vmem_limit_bytes=VMEM_LIMIT
         ),
         name="exchange",
     )(
-        slots, user_mask, own_tiles, params, win_centers, win_exps[None, :], points, weights,
+        slots, user_mask, owner_mask, own_tiles, params, win_centers, win_exps[None, :], points, weights,
         pair_target, pair_source,
     )
-    every = lax.all_gather(weighted, "grid", axis=0, tiled=True)
     return pl.pallas_call(
-        functools.partial(fock_kernel, owners, batches, full),
+        fock_kernel,
         out_shape=jax.ShapeDtypeStruct((held, BLK, width), jnp.float32),
-        in_specs=[smem, smem] + [vmem] * 3,
+        in_specs=[smem, vmem],
         out_specs=vmem,
         compiler_params=pltpu.CompilerParams(vmem_limit_bytes=VMEM_LIMIT),
         name="fock_rows",
-    )(slots, owner_mask, every, all_points, params).reshape(rows_here, width)
+    )(slots, partial).reshape(rows_here, width)
 
 
 def solution(mesh):

time: 137 us -> 82.4 us (0.60)
  the two profiles are of different devices: /device:TPU:0 before, /device:TPU:18 now
where the time goes in v2:
time: 82.4 us; the launch traced here: 82 us
  Pallas kernels  77.4 us (94%)
  other arithmetic  2.46 us (3%)
  local copies, waits for them, and re-layouts  2.17 us (3%)
    pallas_call x1, Pallas kernels, on_device(): pl.pallas_call(functools.partial(exchange_kernel, owners, cols, full), ou...  74.2 us
    pallas_call x1, Pallas kernels, on_device(): pl.pallas_call(fock_kernel, out_shape=jax.ShapeDtypeStruct((held, BLK, wi...  3.18 us

profile of v2, /device:TPU:18, one launch (start us, length us, event | category | flops | bytes accessed | tf_op | source)
XLA Modules:
  0.0 82.0 jit_solution(7897339508499309674)
XLA Ops:
  0.0 0.7 select_reduce_fusion.1
  0.7 0.1 reduce_min.14
  0.8 0.1 reduce_min.18
  0.9 0.1 reduce_max.14
  1.0 0.1 reduce_max.18
  1.2 0.1 copy.13
  1.3 0.6 min.12.slot_ref
  1.9 1.3 %copy.14.points_ref = f32[4,3,128]{2,1,0:T(4,128)} copy(f32[4,3,128]{2,0,1:T(4,128)} %param.15) | data formatting | bytes 12288 | tf_op args[5]
  3.2 1.5 %maximum_bitcast_fusion.params_ref = f32[24,4,128]{2,1,0:T(4,128)} fusion(f32[1,24,128]{2,0,1:T(1,128)} %bitcast.11, f32[3,24,128]{2,0,1:T(4,128)} %bitcast.10), kind=kLoop, calls=%fused_computation | loop fusion | flops 12288 | bytes 98304 | tf_op jit(solution)/shard_map/transpose | solution.py:412
  4.6 74.2 %exchange.1.partial_ref = f32[32,128,128]{2,1,0:T(8,128)} custom-call(s32[32]{0:T(128)} %min.12.slot_ref, f32[1]{0:T(128)} %constant.8.clone.1.mask_ref.owner_mask_ref, f32[1]{0:T(128)} %constant.8.clone.1.mask_ref.owner_mask_ref, bf16[24,128,128]{2,1,0:T(8,128)(2,1)} %bitcast.9, f32[24,4,128]{2,1,0:T(4,128)} %maximum_bitcast_fusion.params_ref, ...), custom_call_target="tpu_custom_call" | custom-call | tf_op jit(solution)/shard_map/exchange/pallas_call | solution.py:413
  78.8 3.2 %fock_rows.1 = f32[24,128,128]{2,1,0:T(8,128)} custom-call(s32[32]{0:T(128)} %min.12.slot_ref, f32[32,128,128]{2,1,0:T(8,128)} %exchange.1.partial_ref), custom_call_target="tpu_custom_call" | custom-call | tf_op jit(solution)/shard_map/fock_rows/pallas_call | solution.py:452
  (1 shorter events, 0.0 us)

commit v3 on v2

--- a/solution.py
+++ b/solution.py
@@ -47,10 +47,10 @@
 
 def exchange_kernel(
     owners, cols, full,
-    slot_ref, mask_ref, owner_mask_ref, density_ref, params_ref, win_c_ref, win_e_ref, points_ref, weights_ref,
+    slot_ref, mask_ref, owner_mask_ref, density_ref, row_c_ref, row_e_ref, win_c_ref, win_e_ref, points_ref, weights_ref,
     target_ref, source_ref,
     partial_ref,
-    every, all_points, tile_send, tile_recv, msg_send, msg_recv, win_buf, spots, pair_scr, source_hot, target_hot, field, parts, parts_recv,
+    params_scr, every, all_points, tile_send, tile_recv, msg_send, msg_recv, win_buf, spots, pair_scr, source_hot, target_hot, field, parts, parts_recv,
     tile_ss, tile_rs, msg_ss, msg_rs, win_ss, win_rs, part_ss, part_rs, every_ss, every_rs,
 ):
     me = lax.axis_index("grid")
@@ -65,6 +65,10 @@
     half_batches = batches // 2
     half = half_batches * pts
 
+    for i in range(params_scr.shape[0]):
+        lanes = slice(i * BLK, (i + 1) * BLK)
+        params_scr[i] = jnp.concatenate([row_c_ref[:, lanes], row_e_ref[:, lanes]], axis=0)
+
     barrier = pltpu.get_barrier_semaphore()
 
     def greet_grid(j, carry):
@@ -142,7 +146,7 @@
         spot = all_points[user]
         for c in range(CAPB):
             block = slot_ref[user * CAPB + c]
-            own = jnp.concatenate([params_ref[block], blank], axis=0).T
+            own = jnp.concatenate([params_scr[block], blank], axis=0).T
             held = [jnp.broadcast_to(own[:, a : a + 1], (BLK, BLK)) for a in range(4)]
             basis = []
             for b in range(h * half_batches, (h + 1) * half_batches):
@@ -168,7 +172,7 @@
         for c in range(CAPB):
             block = slot_ref[peer * CAPB + c]
             tile_to[index, c * BLK : (c + 1) * BLK] = density_ref[block]
-            rows.append(params_ref[block])
+            rows.append(params_scr[block])
         msg_to[index] = jnp.concatenate(rows + [own_points], axis=0)
 
     stage(0, tile_recv, msg_recv, 0)
@@ -314,8 +318,8 @@
             arrived(user, h)
             send_x(user, h)
             send_y(user, h)
+        add_fock(user, 0)
         forward_side(k - 1)
-        add_fock(user, 0)
         add_fock(user, 1)
         add_side(k - 1)
         return carry
@@ -409,13 +413,13 @@
     smem = pl.BlockSpec(memory_space=pltpu.SMEM)
     vmem = pl.BlockSpec(memory_space=pltpu.VMEM)
     own_tiles = density.reshape(held, BLK, width)
-    params = jnp.concatenate([row_centers, row_exps[None, :]], axis=0).reshape(4, held, BLK).transpose(1, 0, 2)
     partial = pl.pallas_call(
         functools.partial(exchange_kernel, owners, cols, full),
         out_shape=jax.ShapeDtypeStruct((owners * CAPB, BLK, width), jnp.float32),
-        in_specs=[smem, smem, smem] + [vmem] * 8,
+        in_specs=[smem, smem, smem] + [vmem] * 9,
         out_specs=vmem,
         scratch_shapes=[
+            pltpu.VMEM((held, 4, BLK), jnp.float32),
             pltpu.VMEM((owners, 2, count // 2, width), jnp.bfloat16),
             pltpu.VMEM((owners, 16, pts), jnp.float32),
             pltpu.VMEM((owners, CAPB * BLK, width), jnp.bfloat16),
@@ -446,7 +450,7 @@
         ),
         name="exchange",
     )(
-        slots, user_mask, owner_mask, own_tiles, params, win_centers, win_exps[None, :], points, weights,
+        slots, user_mask, owner_mask, own_tiles, row_centers, row_exps[None, :], win_centers, win_exps[None, :], points, weights,
         pair_target, pair_source,
     )
     return pl.pallas_call(

time: 82.4 us -> 80.8 us (0.981)
  other arithmetic: 2.46 us -> 1 us
    transpose x1 -> x0, other arithmetic: 1.46 us -> none  [on_device(): jnp.concatenate([row_centers, row_exps[None, :]], axis=0)]
where the time goes in v3:
time: 80.8 us; the launch traced here: 80.5 us
  Pallas kernels  77.4 us (96%)
  local copies, waits for them, and re-layouts  2.15 us (3%)
  other arithmetic  1 us (1%)
    pallas_call x1, Pallas kernels, on_device(): pl.pallas_call(functools.partial(exchange_kernel, owners, cols, full), ou...  74.2 us
    pallas_call x1, Pallas kernels, on_device(): pl.pallas_call(fock_kernel, out_shape=jax.ShapeDtypeStruct((held, BLK, wi...  3.18 us

profile of v3, /device:TPU:18, one launch (start us, length us, event | category | flops | bytes accessed | tf_op | source)
XLA Modules:
  0.0 80.5 jit_solution(11290680346865623100)
XLA Ops:
  0.0 0.7 select_reduce_fusion.1
  0.7 0.1 reduce_min.14
  0.8 0.1 reduce_min.18
  0.9 0.1 reduce_max.14
  1.0 0.1 reduce_max.18
  1.2 0.1 copy.13
  1.3 0.6 min.12.slot_ref
  1.9 1.3 %copy.14.points_ref = f32[4,3,128]{2,1,0:T(4,128)} copy(f32[4,3,128]{2,0,1:T(4,128)} %param.15) | data formatting | bytes 12288 | tf_op args[5]
  3.2 74.2 %exchange.1.partial_ref = f32[32,128,128]{2,1,0:T(8,128)} custom-call(s32[32]{0:T(128)} %min.12.slot_ref, f32[1]{0:T(128)} %constant.8.clone.1.mask_ref.owner_mask_ref, f32[1]{0:T(128)} %constant.8.clone.1.mask_ref.owner_mask_ref, bf16[24,128,128]{2,1,0:T(8,128)(2,1)} %bitcast.6, f32[3,3072]{1,0:T(4,128)} %row_c_ref.1, f32[1,3072]{1,0:T(1,128)} %bitcast.7, ...), custom_call_target="tpu_custom_call" | custom-call | tf_op jit(solution)/shard_map/exchange/pallas_call | solution.py:416
  77.4 3.2 %fock_rows.1 = f32[24,128,128]{2,1,0:T(8,128)} custom-call(s32[32]{0:T(128)} %min.12.slot_ref, f32[32,128,128]{2,1,0:T(8,128)} %exchange.1.partial_ref), custom_call_target="tpu_custom_call" | custom-call | tf_op jit(solution)/shard_map/fock_rows/pallas_call | solution.py:456
  (1 shorter events, 0.0 us)
